TPU v7x, 32 devices: a whole 2x2x4 slice. The times are simulated.
32 devices in a mesh: oi: 8 (over y, x, core), oj: 4 (over z).
Axes of the slice: x: 2, y: 2, z: 4, core: 2. Of those that a mesh axis runs over, the one named last changes fastest.
Arguments:
- amps: bfloat16 [64, 64, 4096], P('oi', 'oj'), may hold values from -6 to 6
- ladder_w: bfloat16 [2016, 2016], P('oj'), may hold values from -0.125 to 0.125
- fock: bfloat16 [64, 64], replicated, may hold values from -0.75 to 0.75
- eps_occ: float32 [64], replicated, may hold values from -2 to -0.3
- eps_pair: float32 [4096], replicated, may hold values from 0.5 to 4
Outputs:
- update: bfloat16 [64, 64, 4096], P('oi', 'oj')
All inputs are finite; a program needn't handle non-finite values.
Results may differ from a plain program's by a relative error of at most 0.0054.
Values may be sent and summed in bfloat16 or wider, within the bound.
A program may use at most 128 MiB of HBM per device.

v0:
```python
import jax
import jax.numpy as jnp
import numpy as np
from jax import lax
from jax.sharding import PartitionSpec as P


def pair_tables(occ):
    first, second = np.triu_indices(occ, 1)
    upper = (first * occ + second).astype(np.int32)
    lower = (second * occ + first).astype(np.int32)
    npairs = upper.shape[0]
    expand = np.full((occ * occ,), 2 * npairs, dtype=np.int32)
    expand[upper] = np.arange(npairs, dtype=np.int32)
    expand[lower] = npairs + np.arange(npairs, dtype=np.int32)
    return (upper, lower, expand)


def divide_out(resid, energies, first_eps, second_eps):
    denom = energies[None, None, :] - first_eps[:, None, None] - second_eps[None, :, None]
    held = lax.optimization_barrier(resid)
    return (held.astype(jnp.float32) / denom).astype(jnp.bfloat16)


def on_device(amps, ladder_w, fock, eps_occ, eps_pair):
    pair_amps = lax.all_to_all(
        lax.all_to_all(amps, "oi", split_axis=2, concat_axis=0, tiled=True),
        "oj",
        split_axis=2,
        concat_axis=1,
        tiled=True,
    )
    occ = pair_amps.shape[0]
    width = pair_amps.shape[2]
    upper, lower, expand = pair_tables(occ)
    flat = pair_amps.reshape(occ * occ, width)
    anti = (flat[upper].astype(jnp.float32) - flat[lower].astype(jnp.float32)).astype(jnp.bfloat16)
    contract = (((0,), (0,)), ((), ()))
    whole_w = lax.all_gather(ladder_w, "oj", axis=0, tiled=True)
    offset = (lax.axis_index("oi") * lax.axis_size("oj") + lax.axis_index("oj")) * width
    ladder = lax.dot_general(
        whole_w, anti[:, 0 : 0 + width], contract, preferred_element_type=jnp.float32
    )
    mixed = jnp.einsum("ikp,kj->ijp", pair_amps, fock, preferred_element_type=jnp.float32)
    filler = jnp.zeros((1, width), jnp.float32)
    full = jnp.concatenate([ladder, -ladder, filler], axis=0)[expand].reshape(occ, occ, width)
    resid = (full - (mixed - jnp.transpose(mixed, (1, 0, 2)))).astype(jnp.bfloat16)
    energies = lax.dynamic_slice_in_dim(eps_pair, offset + 0, width, 0)
    outgoing = divide_out(resid, energies, eps_occ, eps_occ).reshape(occ, occ, 1, 1, width)
    landed = lax.all_to_all(
        lax.all_to_all(outgoing, "oi", split_axis=0, concat_axis=2, tiled=True),
        "oj",
        split_axis=1,
        concat_axis=3,
        tiled=True,
    )
    rows_i = landed.shape[0]
    rows_j = landed.shape[1]
    arrived = landed.reshape(rows_i, rows_j, landed.shape[2] * landed.shape[3] * width)
    return arrived


def solution(mesh):
    in_specs = (P("oi", "oj", None), P("oj", None), P(), P(), P())
    out_specs = P("oi", "oj", None)
    return jax.shard_map(
        on_device, mesh=mesh, in_specs=in_specs, out_specs=out_specs, check_vma=False
    )
```

profile of v0, /device:TPU:0, one launch (start us, length us, event | category | flops | bytes accessed | tf_op | source)
XLA Modules:
  0.0 268.4 jit_solution(13245304063017883715)
XLA Ops:
  6.5 0.0 copy-start
  6.5 0.0 copy-start.1
  6.5 0.0 all-gather.2.cloned.1.call-start
  6.5 0.7 all-gather.2.cloned.1.call-update
  7.3 0.5 copy-done.1
  7.8 7.3 %copy.41 = bf16[8,16,4096]{1,0,2:T(8,128)(2,1)} copy(bf16[8,16,4096]{2,1,0:T(8,128)(2,1)S(1)} %copy-done.1) | data formatting | bytes 2097152 | tf_op args[0]
  15.1 10.8 %reshape.73 = bf16[8,2,32768]{2,1,0:T(2,128)(2,1)S(1)} reshape(bf16[4096,8,16]{2,1,0:T(8,128)(2,1)} %bitcast.45) | data formatting | bytes 2097152
  25.9 20.3 %all_to_all.69 = bf16[8,2,32768]{2,1,0:T(2,128)(2,1)S(1)} all-to-all(bf16[8,2,32768]{2,1,0:T(2,128)(2,1)S(1)} %reshape.73), channel_id=1, replica_groups=mesh['oi'=8,'oj'=4] {'oi'}, dimensions={0} | all-to-all | bytes 2097152 | tf_op jit(solution)/shard_map/all_to_all | solution.py:27
  46.2 7.5 %reshape.74 = bf16[4096,8,16]{2,1,0:T(8,128)(2,1)} reshape(bf16[8,2,32768]{2,1,0:T(2,128)(2,1)S(1)} %all_to_all.69) | data formatting | bytes 2097152
  53.7 8.3 %copy.43 = bf16[8,8,16,512]{3,2,1,0:T(8,128)(2,1)S(1)} copy(bf16[8,8,16,512]{2,1,3,0:T(8,128)(2,1)} %bitcast.44) | data formatting | bytes 2097152 | tf_op jit(solution)/shard_map/all_to_all | solution.py:27
  62.0 2.7 copy.44
  64.7 0.0 copy-start.4
  64.7 0.0 copy-start.3
  64.7 0.0 copy-start.2
  64.7 0.0 copy-start.5
  64.8 2.7 reshape.75
  67.4 4.8 %all-to-all-start.1 = ((bf16[4,2,65536]{2,1,0:T(2,128)(2,1)}), bf16[4,2,65536]{2,1,0:T(2,128)(2,1)S(1)}, u32[]{:S(2)}, u32[]{:S(2)}) async-start(bf16[4,2,65536]{2,1,0:T(2,128)(2,1)} %reshape.75), calls=%async_computation.1 | async-start | bytes 2097152 | tf_op jit(solution)/shard_map/all_to_all | solution.py:26
  72.2 0.8 dynamic_slice.3
  73.0 0.1 pad.2.clone
  73.1 0.0 copy-done.4
  73.1 0.0 copy-done.3
  73.1 0.0 copy-done.2
  73.1 0.0 copy-done.5
  73.2 0.1 broadcast_subtract_fusion
  73.2 53.4 %all-to-all-done.1 = bf16[4,2,65536]{2,1,0:T(2,128)(2,1)S(1)} async-done(((bf16[4,2,65536]{2,1,0:T(2,128)(2,1)}), bf16[4,2,65536]{2,1,0:T(2,128)(2,1)S(1)}, u32[]{:S(2)}, u32[]{:S(2)}) %all-to-all-start.1) | async-done | bytes 1048608 | tf_op jit(solution)/shard_map/all_to_all | solution.py:26
  126.7 1.4 reshape.76
  128.1 2.8 %copy.57 = bf16[64,16,4,128]{3,2,1,0:T(4,128)(2,1)S(1)} copy(bf16[64,16,4,128]{0,1,3,2:T(8,128)(2,1)S(1)} %bitcast.47) | data formatting | bytes 2097152 | tf_op jit(solution)/shard_map/all_to_all | solution.py:26
  130.9 0.3 copy.46
  131.1 6.3 %gather_fusion = bf16[2016,128]{1,0:T(8,128)(2,1)S(1)} fusion(bf16[4096,128]{1,0:T(8,128)(2,1)S(1)} %bitcast.41, s32[2048]{0:T(1024)S(1)} %pad_clamp_fusion.1), kind=kCustom, calls=%fused_computation | custom fusion | bytes 1040256 | tf_op jit(solution)/shard_map/gather | solution.py:37
  137.5 6.3 %gather_fusion.1 = bf16[2016,128]{1,0:T(8,128)(2,1)S(1)} fusion(bf16[4096,128]{1,0:T(8,128)(2,1)S(1)} %bitcast.42, s32[2048]{0:T(1024)S(1)} %pad_clamp_fusion), kind=kCustom, calls=%fused_computation.1 | custom fusion | bytes 1040256 | tf_op jit(solution)/shard_map/gather | solution.py:37
  143.8 0.0 copy-done
  143.8 1.8 fusion.3
  145.6 35.9 %all-gather.2.cloned.1.call-done = bf16[2016,2016]{1,0:T(8,128)(2,1)} async-done(((bf16[504,2016]{1,0:T(8,128)(2,1)}), bf16[2016,2016]{1,0:T(8,128)(2,1)}) %all-gather.2.cloned.1.call-update) | async-done | bytes 8128528 | tf_op jit(solution)/shard_map/all_gather | solution.py:39
  181.5 6.8 %fusion.5 = (f32[2016,128]{1,0:T(8,128)S(1)}, f32[2016,128]{1,0:T(8,128)S(1)}) fusion(bf16[2016,2016]{1,0:T(8,128)(2,1)} %all-gather.2.cloned.1.call-done, bf16[2016,128]{1,0:T(8,128)(2,1)S(1)} %gather_fusion.1, bf16[2016,128]{1,0:T(8,128)(2,1)S(1)} %gather_fusion), kind=kOutput, calls=%fused_computation.18 | convolution fusion | flops 1041739776 | bytes 11225088 | tf_op jit(solution)/shard_map/dot_general | solution.py:41
  188.3 3.1 %maximum_maximum_fusion = f32[4033,128]{1,0:T(8,128)S(1)} fusion(f32[2016,128]{1,0:T(8,128)S(1)} %get-tuple-element.5, f32[2016,128]{1,0:T(8,128)S(1)} %get-tuple-element.6, f32[4033]{0:T(1024)S(1)} %pad.2.clone), kind=kLoop, calls=%fused_computation.8 | loop fusion | flops 1032448 | bytes 4145412 | tf_op jit(solution)/shard_map/concatenate | solution.py:46
  191.4 14.1 %gather_fusion.2 = f32[4096,128]{1,0:T(8,128)} fusion(f32[4033,128]{1,0:T(8,128)S(1)} %maximum_maximum_fusion, s32[4096]{0:T(1024)S(1)} %broadcast_clamp_fusion), kind=kCustom, calls=%fused_computation.2 | custom fusion | bytes 4210688 | tf_op jit(solution)/shard_map/gather | solution.py:46
  205.5 5.2 %fusion.1 = bf16[64,64,128]{2,0,1:T(8,128)(2,1)S(1)} fusion(f32[64,64,128]{2,0,1:T(8,128)} %fusion.3, f32[64,64,128]{2,1,0:T(8,128)} %bitcast.48), kind=kLoop, calls=%fused_computation.6 | loop fusion | flops 1572864 | bytes 5242880 | tf_op jit(solution)/shard_map/convert_element_type | solution.py:47
  210.7 0.4 fusion.2
  211.2 0.7 copy.51
  211.9 18.8 %all_to_all.70 = bf16[64,64,1,1,128]{4,1,3,2,0:T(8,128)(2,1)S(1)} all-to-all(bf16[64,64,1,1,128]{4,1,3,2,0:T(8,128)(2,1)S(1)} %copy.51), channel_id=1, replica_groups=mesh['oi'=8,'oj'=4] {'oi'}, dimensions={0} | all-to-all | bytes 2097152 | tf_op jit(solution)/shard_map/all_to_all | solution.py:51
  230.7 0.7 copy.62
  231.4 27.8 %all_to_all.71 = bf16[8,64,8,1,128]{4,0,2,3,1:T(8,128)(2,1)S(1)} all-to-all(bf16[8,64,8,1,128]{4,0,2,3,1:T(8,128)(2,1)S(1)} %bitcast.52), channel_id=1, replica_groups=mesh['oi'=8,'oj'=4] {'oj'}, dimensions={1} | all-to-all | bytes 2097152 | tf_op jit(solution)/shard_map/all_to_all | solution.py:50
  259.1 0.8 copy.53
  260.0 1.6 reshape.46
  (3 shorter events, 0.0 us)
Async XLA Ops:
  6.5 137.3 %copy-start = (bf16[64,64]{1,0:T(8,128)(2,1)S(1)}, bf16[64,64]{1,0:T(8,128)(2,1)}, u32[]{:S(2)}) copy-start(bf16[64,64]{1,0:T(8,128)(2,1)} %param.13) | copy-start | bytes 24580
  6.5 1.2 copy-start.1
  6.5 175.0 %all-gather.2.cloned.1.call-start = ((), (), s32[]{:S(2)}) async-start(), calls=%async_computation.4 | async-start | bytes 10321920 | tf_op jit(solution)/shard_map/all_gather | solution.py:39
  64.7 8.4 %copy-start.4 = (s32[2016]{0:T(1024)S(1)}, s32[2016]{0:T(1024)}, u32[]{:S(2)}) copy-start(s32[2016]{0:T(1024)} %constant.39) | copy-start | bytes 24196
  64.7 8.4 %copy-start.3 = (s32[2016]{0:T(1024)S(1)}, s32[2016]{0:T(1024)}, u32[]{:S(2)}) copy-start(s32[2016]{0:T(1024)} %constant.40) | copy-start | bytes 24196
  64.7 8.4 %copy-start.2 = (s32[4096]{0:T(1024)S(1)}, s32[4096]{0:T(1024)}, u32[]{:S(2)}) copy-start(s32[4096]{0:T(1024)} %constant.41) | copy-start | bytes 49156
  64.7 8.4 %copy-start.5 = (f32[64]{0:T(128)S(1)}, f32[64]{0:T(128)}, u32[]{:S(2)}) copy-start(f32[64]{0:T(128)} %param.14) | copy-start | bytes 772
  67.4 59.2 %all-to-all-start.1 = ((bf16[4,2,65536]{2,1,0:T(2,128)(2,1)}), bf16[4,2,65536]{2,1,0:T(2,128)(2,1)S(1)}, u32[]{:S(2)}, u32[]{:S(2)}) async-start(bf16[4,2,65536]{2,1,0:T(2,128)(2,1)} %reshape.75), calls=%async_computation.1 | async-start | bytes 2097152 | tf_op jit(solution)/shard_map/all_to_all | solution.py:26
Sparse Core Ops, SparseCore 0:
  8.9 172.5 all-gather.1
where the time goes:
time: 269 us; the launch traced here: 268 us
  waiting for transfers between devices  90 us (33%)
  local copies, waits for them, and re-layouts  75.7 us (28%)
  blocking collectives  66.9 us (25%)
  between operations  13.6 us (5%)
  other arithmetic  8.86 us (3%)
  matrix products  8.58 us (3%)
  starting transfers between devices  4.83 us (2%)
    all_to_all x1, waiting for transfers between devices, on_device(): lax.all_to_all(lax.all_to_all(amps, 'oi', split_axis=2, concat_axis=0, ti...  53.4 us
    all_gather x1, waiting for transfers between devices, on_device(): whole_w = lax.all_gather(ladder_w, 'oj', axis=0, tiled=True)  35.9 us
    unnamed x17, local copies, waits for them, and re-layouts  30.3 us
    all_to_all x1, blocking collectives, on_device(): lax.all_to_all(lax.all_to_all(outgoing, 'oi', split_axis=0, concat_axis=2...  27.8 us
    all_to_all x1, blocking collectives, on_device(): lax.all_to_all(amps, 'oi', split_axis=2, concat_axis=0, tiled=True)  20.3 us
    all_to_all x1, blocking collectives, on_device(): lax.all_to_all(outgoing, 'oi', split_axis=0, concat_axis=2, tiled=True)  18.8 us
    gather x1, local copies, waits for them, and re-layouts, on_device(): jnp.concatenate([ladder, -ladder, filler], axis=0)[expand]  14.1 us
    all_to_all x2, local copies, waits for them, and re-layouts, on_device(): lax.all_to_all(amps, 'oi', split_axis=2, concat_axis=0, tiled=True)  11 us
  transfers between devices with their start and end apart: 2, of which 2 were waited for; matrix products, arithmetic and copies ran while one was open for 22% of the time, Pallas kernels for 0%

commit v1 on v0

--- a/solution.py
+++ b/solution.py
@@ -1,8 +1,17 @@
+import functools
+
 import jax
 import jax.numpy as jnp
 import numpy as np
 from jax import lax
+from jax.experimental import pallas as pl
+from jax.experimental.pallas import tpu as pltpu
 from jax.sharding import PartitionSpec as P
+
+MESH = pl.DeviceIdType.MESH
+LANES = 128
+F32 = jnp.float32
+BF16 = jnp.bfloat16
 
 
 def pair_tables(occ):
@@ -22,7 +31,7 @@
     return (held.astype(jnp.float32) / denom).astype(jnp.bfloat16)
 
 
-def on_device(amps, ladder_w, fock, eps_occ, eps_pair):
+def with_collectives(amps, ladder_w, fock, eps_occ, eps_pair):
     pair_amps = lax.all_to_all(
         lax.all_to_all(amps, "oi", split_axis=2, concat_axis=0, tiled=True),
         "oj",
@@ -59,8 +68,277 @@
     arrived = landed.reshape(rows_i, rows_j, landed.shape[2] * landed.shape[3] * width)
     return arrived
 
+def spot(first, second):
+    return (first, second)
+
+
+def greet_all(noi, noj):
+    n = noi * noj
+    me = lax.axis_index("oi") * noj + lax.axis_index("oj")
+    barrier = pltpu.get_barrier_semaphore()
+
+    @pl.loop(1, n)
+    def _(t):
+        peer = lax.rem(me + t, n)
+        pl.semaphore_signal(
+            barrier, inc=1, device_id=spot(peer // noj, lax.rem(peer, noj)), device_id_type=MESH
+        )
+
+    pl.semaphore_wait(barrier, n - 1)
+    return me
+
+
+def gather_kernel(noi, noj, amps, wpad, pair, wfull, asend, arecv, zsend, zrecv, xsend, xrecv,
+                  csend, crecv, own):
+    n = noi * noj
+    bi, bj = amps.shape[0], amps.shape[1]
+    nq = noi // 2
+    rows = wpad.shape[0] // nq
+    half = wpad.shape[1] // 2
+    oi, oj = lax.axis_index("oi"), lax.axis_index("oj")
+    q, core = oi // 2, lax.rem(oi, 2)
+    me = greet_all(noi, noj)
+
+    def part(ref, quarter, side):
+        return ref.at[pl.ds(pl.multiple_of(quarter * rows, rows), rows),
+                      pl.ds(pl.multiple_of(side * half, half), half)]
+
+    def slot(shard, quarter, side):
+        return part(wfull.at[shard], quarter, side)
+
+    def z_copy(dz):
+        return pltpu.make_async_remote_copy(
+            src_ref=part(wpad, q, core), dst_ref=slot(oj, q, core),
+            send_sem=zsend.at[dz], recv_sem=zrecv.at[dz],
+            device_id=spot(oi, lax.rem(oj + dz, noj)), device_id_type=MESH)
+
+    def x_copy(dz, dq):
+        s = lax.rem(oj + noj - dz, noj)
+        return pltpu.make_async_remote_copy(
+            src_ref=slot(s, q, core), dst_ref=slot(s, q, core),
+            send_sem=xsend.at[dz, dq], recv_sem=xrecv.at[dz, dq],
+            device_id=spot(lax.rem(q + dq, nq) * 2 + core, oj), device_id_type=MESH)
+
+    def c_copy(dz, dq):
+        s = lax.rem(oj + noj - dz, noj)
+        quarter = lax.rem(q + nq - dq, nq)
+        return pltpu.make_async_remote_copy(
+            src_ref=slot(s, quarter, core), dst_ref=slot(s, quarter, core),
+            send_sem=csend.at[dz, dq], recv_sem=crecv.at[dz, dq],
+            device_id=spot(q * 2 + 1 - core, oj), device_id_type=MESH)
+
+    def a_copy(t):
+        peer = lax.rem(me + t, n)
+        return pltpu.make_async_remote_copy(
+            src_ref=amps.at[:, :, pl.ds(pl.multiple_of(peer * LANES, LANES), LANES)],
+            dst_ref=pair.at[pl.ds(oi * bi, bi), pl.ds(pl.multiple_of(oj * bj, bj), bj), :],
+            send_sem=asend.at[t], recv_sem=arecv.at[t],
+            device_id=spot(peer // noj, lax.rem(peer, noj)), device_id_type=MESH)
+
+    for dz in range(1, noj):
+        z_copy(dz).start()
+
+    @pl.loop(1, n)
+    def _(t):
+        a_copy(t).start()
+
+    mine = pltpu.make_async_copy(
+        amps.at[:, :, pl.ds(pl.multiple_of(me * LANES, LANES), LANES)],
+        pair.at[pl.ds(oi * bi, bi), pl.ds(pl.multiple_of(oj * bj, bj), bj), :], own.at[0])
+    mine.start()
+    whole = pltpu.make_async_copy(wpad, wfull.at[oj], own.at[1])
+    whole.start()
+
+    for dz in range(1, noj):
+        z_copy(dz).wait_recv()
+        for dq in range(1, nq):
+            x_copy(dz, dq).start()
+        c_copy(dz, 0).start()
+    for dz in range(1, noj):
+        for dq in range(1, nq):
+            x_copy(dz, dq).wait_recv()
+            c_copy(dz, dq).start()
+    mine.wait()
+    whole.wait()
+    for dz in range(1, noj):
+        z_copy(dz).wait_send()
+        for dq in range(nq):
+            if dq:
+                x_copy(dz, dq).wait_send()
+            c_copy(dz, dq).wait()
+
+    @pl.loop(1, n)
+    def _(t):
+        a_copy(t).wait()
+
+
+def gather(noi, noj, amps, wpad, occ):
+    nq = noi // 2
+    dma = pltpu.SemaphoreType.DMA
+    return pl.pallas_call(
+        functools.partial(gather_kernel, noi, noj),
+        out_shape=(
+            jax.ShapeDtypeStruct((occ, occ, LANES), BF16),
+            jax.ShapeDtypeStruct((noj,) + wpad.shape, BF16),
+        ),
+        in_specs=[pl.BlockSpec(memory_space=pl.ANY)] * 2,
+        out_specs=(pl.BlockSpec(memory_space=pl.ANY),) * 2,
+        scratch_shapes=[
+            dma((noi * noj,)), dma((noi * noj,)), dma((noj,)), dma((noj,)),
+            dma((noj, nq)), dma((noj, nq)), dma((noj, nq)), dma((noj, nq)), dma((2,)),
+        ],
+        compiler_params=pltpu.CompilerParams(collective_id=0, has_side_effects=True),
+    )(amps, wpad)
+
+
+def spread_kernel(noi, noj, upd, out, send, recv, own):
+    n = noi * noj
+    bi, bj = out.shape[0], out.shape[1]
+    me = greet_all(noi, noj)
+
+    def block(peer):
+        return upd.at[pl.ds((peer // noj) * bi, bi),
+                      pl.ds(pl.multiple_of(lax.rem(peer, noj) * bj, bj), bj), :]
+
+    here = out.at[:, :, pl.ds(pl.multiple_of(me * LANES, LANES), LANES)]
+
+    def copy(t):
+        peer = lax.rem(me + t, n)
+        return pltpu.make_async_remote_copy(
+            src_ref=block(peer), dst_ref=here, send_sem=send.at[t], recv_sem=recv.at[t],
+            device_id=spot(peer // noj, lax.rem(peer, noj)), device_id_type=MESH)
+
+    @pl.loop(1, n)
+    def _(t):
+        copy(t).start()
+
+    mine = pltpu.make_async_copy(block(me), here, own)
+    mine.start()
+    mine.wait()
+
+    @pl.loop(1, n)
+    def _(t):
+        copy(t).wait()
+
+
+def spread(noi, noj, upd, bi, bj):
+    dma = pltpu.SemaphoreType.DMA
+    return pl.pallas_call(
+        functools.partial(spread_kernel, noi, noj),
+        out_shape=jax.ShapeDtypeStruct((bi, bj, noi * noj * LANES), BF16),
+        in_specs=[pl.BlockSpec(memory_space=pl.ANY)],
+        out_specs=pl.BlockSpec(memory_space=pl.ANY),
+        scratch_shapes=[dma((noi * noj,)), dma((noi * noj,)), dma],
+        compiler_params=pltpu.CompilerParams(collective_id=1, has_side_effects=True),
+    )(upd)
+
+
+def pair_start(occ, k):
+    return k * (occ - 1) - k * (k - 1) // 2
+
+
+def pack_anti(occ, shard, padded, wide, packed):
+    nshards = packed.shape[0] // padded
+    for s in range(nshards):
+        packed[s * padded + shard:(s + 1) * padded, :] = jnp.zeros((padded - shard, LANES), F32)
+    for k in range(occ - 1):
+        row = wide[k * occ:(k + 1) * occ, :]
+        col = wide[pl.ds(k, occ, stride=occ), :]
+        diff = row - col
+        at, end = pair_start(occ, k), pair_start(occ, k + 1)
+        base = k + 1 - at
+        while at < end:
+            s = at // shard
+            stop = min(end, (s + 1) * shard)
+            lift = s * (padded - shard)
+            packed[at + lift:stop + lift, :] = diff[at + base:stop + base, :]
+            at = stop
+
+
+def compute_kernel(occ, shard, padded, noj, pair, w, fock, eps_row, energies, upd, wide, mixed,
+                   packed, lad, rf):
+    me = lax.axis_index("oi") * noj + lax.axis_index("oj")
+    flipped = fock[...].astype(F32).T.astype(BF16)
+
+    @pl.loop(0, occ)
+    def _(i):
+        block = pair[i]
+        at = pl.ds(pl.multiple_of(i * occ, occ), occ)
+        wide[at, :] = block.astype(F32)
+        mixed[at, :] = jnp.dot(flipped, block, preferred_element_type=F32)
+
+    pack_anti(occ, shard, padded, wide, packed)
+    left = packed[...].T.astype(BF16)
+    step = 256
+    for c in range(0, w.shape[1], step):
+        lt = jnp.dot(left, w[:, c:c + step], preferred_element_type=F32)
+        lad[c:c + step, :] = lt.T
+    finish(occ, eps_row, energies[pl.ds(me, 1), :], lad, mixed, rf, upd)
+
+
+def finish(occ, eps_row, energy, lad, mixed, rf, upd):
+    for i in range(occ):
+        if i == occ - 1:
+            break
+        row = mixed[i * occ:(i + 1) * occ, :]
+        col = mixed[pl.ds(i, occ, stride=occ), :]
+        at, n = pair_start(occ, i), occ - 1 - i
+        diff = (row - col)[i + 1:, :]
+        rf[i * occ + i + 1:(i + 1) * occ, :] = lad[at:at + n, :] - diff
+    second = jnp.broadcast_to(eps_row[...], (LANES, LANES)).T[:occ, :]
+    index = lax.broadcasted_iota(jnp.int32, (occ, LANES), 0)
+    for i in range(occ):
+        row = rf[i * occ:(i + 1) * occ, :]
+        col = rf[pl.ds(i, occ, stride=occ), :]
+        value = jnp.where(index > i, row, jnp.where(index < i, -col, 0.0))
+        denom = (energy - eps_row[0:1, i:i + 1]) - second
+        value = value.astype(BF16).astype(F32)
+        upd[i] = (value / denom).astype(BF16)
+
+
+def compute(noj, shard, padded, pair, w, fock, eps_row, energies):
+    occ = pair.shape[0]
+    vmem = pl.BlockSpec(memory_space=pltpu.VMEM)
+    return pl.pallas_call(
+        functools.partial(compute_kernel, occ, shard, padded, noj),
+        out_shape=jax.ShapeDtypeStruct((occ, occ, LANES), BF16),
+        in_specs=[vmem] * 5,
+        out_specs=vmem,
+        scratch_shapes=[
+            pltpu.VMEM((occ * occ, LANES), F32), pltpu.VMEM((occ * occ, LANES), F32),
+            pltpu.VMEM((w.shape[0], LANES), F32), pltpu.VMEM((w.shape[1], LANES), F32),
+            pltpu.VMEM((occ * occ, LANES), F32),
+        ],
+        compiler_params=pltpu.CompilerParams(vmem_limit_bytes=40 * 2**20),
+    )(pair, w, fock, eps_row, energies)
+
+
+def up_to(value, unit):
+    return -(-value // unit) * unit
+
+
+def with_kernels(noi, noj, amps, ladder_w, fock, eps_occ, eps_pair):
+    occ = amps.shape[0] * noi
+    shard, cols = ladder_w.shape
+    padded = up_to(shard, 16 * noi // 2)
+    wpad = jnp.pad(ladder_w, ((0, padded - shard), (0, up_to(cols, 256) - cols)))
+    pair, wfull = gather(noi, noj, amps, wpad, occ)
+    eps_row = jnp.pad(eps_occ, (0, LANES - occ)).reshape(1, LANES)
+    upd = compute(noj, shard, padded, pair, wfull.reshape(noj * padded, wpad.shape[1]), fock,
+                  eps_row, eps_pair.reshape(noi * noj, LANES))
+    return spread(noi, noj, upd, amps.shape[0], amps.shape[1])
+
 
 def solution(mesh):
+    noi, noj = mesh.shape["oi"], mesh.shape["oj"]
+
+    def on_device(amps, *rest):
+        fits = amps.shape[1] % 16 == 0 and amps.shape[2] == noi * noj * LANES
+        fits = fits and noi % 2 == 0 and amps.shape[0] * noi <= LANES
+        if fits:
+            return with_kernels(noi, noj, amps, *rest)
+        return with_collectives(amps, *rest)
+
     in_specs = (P("oi", "oj", None), P("oj", None), P(), P(), P())
     out_specs = P("oi", "oj", None)
     return jax.shard_map(

time: 269 us -> 126 us (0.47)
  Pallas kernels: 0 us -> 114 us
  waiting for transfers between devices: 90 us -> 0 us
  blocking collectives: 66.9 us -> 0 us
  local copies, waits for them, and re-layouts: 75.7 us -> 11.1 us
  between operations: 13.6 us -> 0.08 us
  other arithmetic: 8.86 us -> 0 us
  matrix products: 8.58 us -> 0 us
  starting transfers between devices: 4.83 us -> 0 us
    pallas_call x0 -> x3, Pallas kernels: none -> 114 us  [the longest x1 74.5 us: gather(): pl.pallas_call(functools.partial(gather_kernel, noi, noj), out_shape=(jax...]
    all_to_all x3 -> x0, blocking collectives: 66.9 us -> none  [the longest x1 27.8 us: on_device(): lax.all_to_all(lax.all_to_all(outgoing, 'oi', split_axis=0, concat_axis=2...]
    all_to_all x1 -> x0, waiting for transfers between devices: 53.4 us -> none  [on_device(): lax.all_to_all(lax.all_to_all(amps, 'oi', split_axis=2, concat_axis=0, ti...]
    all_gather x1 -> x0, waiting for transfers between devices: 35.9 us -> none  [on_device(): whole_w = lax.all_gather(ladder_w, 'oj', axis=0, tiled=True)]
    gather x3 -> x0, local copies, waits for them, and re-layouts: 26.8 us -> none  [the longest x1 14.1 us: on_device(): jnp.concatenate([ladder, -ladder, filler], axis=0)[expand]]
    unnamed x17 -> x13, local copies, waits for them, and re-layouts: 30.3 us -> 7.86 us
    all_to_all x6 -> x0, local copies, waits for them, and re-layouts: 15.5 us -> none  [the longest x2 11 us: on_device(): lax.all_to_all(amps, 'oi', split_axis=2, concat_axis=0, tiled=True)]
    dot_general x2 -> x0, matrix products: 8.58 us -> none  [the longest x1 6.78 us: on_device(): lax.dot_general(whole_w, anti[:, 0:0 + width], contract, preferred_elemen...]
  transfers between devices with their start and end apart: 2 -> 0, of which waited for: 2 -> 0; matrix products, arithmetic and copies ran while one was open for 22% -> 0% of each run, Pallas kernels for 0% -> 0%
where the time goes in v1:
time: 126 us; the launch traced here: 125 us
  Pallas kernels  114 us (90%)
  local copies, waits for them, and re-layouts  11.1 us (9%)
    pallas_call x1, Pallas kernels, gather(): pl.pallas_call(functools.partial(gather_kernel, noi, noj), out_shape=(jax...  74.5 us
    pallas_call x1, Pallas kernels, spread(): pl.pallas_call(functools.partial(spread_kernel, noi, noj), out_shape=jax....  27.5 us
    pallas_call x1, Pallas kernels, compute(): pl.pallas_call(functools.partial(compute_kernel, occ, shard, padded, noj)...  12.1 us
    unnamed x13, local copies, waits for them, and re-layouts  7.86 us
    pad x1, local copies, waits for them, and re-layouts, with_kernels(): jnp.pad(ladder_w, ((0, padded - shard), (0, up_to(cols, 256) - cols)))  3.23 us

profile of v1, /device:TPU:0, one launch (start us, length us, event | category | flops | bytes accessed | tf_op | source)
XLA Modules:
  0.0 125.3 jit_solution(6976731710485105880)
XLA Ops:
  0.0 3.2 %pad.8.wpad = bf16[512,2048]{1,0:T(8,128)(2,1)} pad(bf16[504,2016]{1,0:T(8,128)(2,1)} %param.6, bf16[]{:T(256)} %constant.3.clone.1), padding=0_8x0_32 | pad | bytes 4129282 | tf_op jit(solution)/shard_map/jit(_pad)/pad | solution.py:324
  3.2 0.0 copy-start.5
  3.2 0.0 copy-start.3
  3.2 0.0 copy-start.4
  3.2 74.5 %shard_map.55 = (bf16[64,64,128]{2,1,0:T(8,128)(2,1)}, bf16[4,512,2048]{2,1,0:T(8,128)(2,1)}) custom-call(bf16[8,16,4096]{2,1,0:T(8,128)(2,1)} %amps.1, bf16[512,2048]{1,0:T(8,128)(2,1)} %pad.8.wpad), custom_call_target="tpu_custom_call" | custom-call | tf_op jit(solution)/shard_map/pallas_call | solution.py:178
  77.7 0.0 copy-done.5
  77.8 0.0 copy-done.3
  77.8 0.0 copy-done.4
  77.8 0.0 copy-start
  77.8 3.4 %copy-done = bf16[4,512,2048]{2,1,0:T(8,128)(2,1)S(1)} copy-done((bf16[4,512,2048]{2,1,0:T(8,128)(2,1)S(1)}, bf16[4,512,2048]{2,1,0:T(8,128)(2,1)}, u32[]{:S(2)}) %copy-start) | copy-done | bytes 8388632
  81.2 0.0 copy-start.2
  81.2 1.2 copy-done.2
  82.4 12.1 %shard_map.56.upd = bf16[64,64,128]{2,1,0:T(8,128)(2,1)S(1)} custom-call(bf16[64,64,128]{2,1,0:T(8,128)(2,1)S(1)} %copy-done.2, bf16[2048,2048]{1,0:T(8,128)(2,1)S(1)} %bitcast.4, bf16[64,64]{1,0:T(8,128)(2,1)S(1)} %copy-done.3, f32[1,128]{1,0:T(1,128)S(1)} %pad_bitcast_fusion.eps_row, f32[32,128]{1,0:T(8,128)S(1)} %bitcast.5), custom_call_target="tpu_custom_call" | custom-call | tf_op jit(solution)/shard_map/pallas_call | solution.py:302
  94.5 0.0 copy-start.1
  94.5 1.0 copy-done.1
  95.4 27.5 %shard_map.57 = bf16[8,16,4096]{2,1,0:T(8,128)(2,1)} custom-call(bf16[64,64,128]{2,1,0:T(8,128)(2,1)} %copy-done.1), custom_call_target="tpu_custom_call" | custom-call | tf_op jit(solution)/shard_map/pallas_call | solution.py:226
  123.0 2.3 %copy.7 = bf16[8,16,4096]{2,1,0:T(8,128)(2,1)} copy(bf16[8,16,4096]{2,1,0:T(8,128)(2,1)} %shard_map.57) | data formatting | bytes 2097152
  (1 shorter events, 0.0 us)
Async XLA Ops:
  3.2 74.5 %copy-start.5 = (f32[64]{0:T(128)S(1)}, f32[64]{0:T(128)}, u32[]{:S(2)}) copy-start(f32[64]{0:T(128)} %param.8) | copy-start | bytes 772
  3.2 74.5 %copy-start.3 = (bf16[64,64]{1,0:T(8,128)(2,1)S(1)}, bf16[64,64]{1,0:T(8,128)(2,1)}, u32[]{:S(2)}) copy-start(bf16[64,64]{1,0:T(8,128)(2,1)} %fock.1) | copy-start | bytes 24580
  3.2 74.5 %copy-start.4 = (f32[4096]{0:T(1024)S(1)}, f32[4096]{0:T(1024)}, u32[]{:S(2)}) copy-start(f32[4096]{0:T(1024)} %param.9) | copy-start | bytes 49156
  77.8 3.4 %copy-start = (bf16[4,512,2048]{2,1,0:T(8,128)(2,1)S(1)}, bf16[4,512,2048]{2,1,0:T(8,128)(2,1)}, u32[]{:S(2)}) copy-start(bf16[4,512,2048]{2,1,0:T(8,128)(2,1)} %get-tuple-element.8) | copy-start | bytes 25165828
  81.2 1.2 copy-start.2
  94.5 1.0 copy-start.1

commit v2 on v0

--- a/solution.py
+++ b/solution.py
@@ -1,8 +1,17 @@
+import functools
+
 import jax
 import jax.numpy as jnp
 import numpy as np
 from jax import lax
+from jax.experimental import pallas as pl
+from jax.experimental.pallas import tpu as pltpu
 from jax.sharding import PartitionSpec as P
+
+MESH = pl.DeviceIdType.MESH
+LANES = 128
+F32 = jnp.float32
+BF16 = jnp.bfloat16
 
 
 def pair_tables(occ):
@@ -22,7 +31,7 @@
     return (held.astype(jnp.float32) / denom).astype(jnp.bfloat16)
 
 
-def on_device(amps, ladder_w, fock, eps_occ, eps_pair):
+def with_collectives(amps, ladder_w, fock, eps_occ, eps_pair):
     pair_amps = lax.all_to_all(
         lax.all_to_all(amps, "oi", split_axis=2, concat_axis=0, tiled=True),
         "oj",
@@ -59,8 +68,311 @@
     arrived = landed.reshape(rows_i, rows_j, landed.shape[2] * landed.shape[3] * width)
     return arrived
 
+def spot(first, second):
+    return (first, second)
+
+
+def greet_all(noi, noj):
+    n = noi * noj
+    me = lax.axis_index("oi") * noj + lax.axis_index("oj")
+    barrier = pltpu.get_barrier_semaphore()
+
+    @pl.loop(1, n)
+    def _(t):
+        peer = lax.rem(me + t, n)
+        pl.semaphore_signal(
+            barrier, inc=1, device_id=spot(peer // noj, lax.rem(peer, noj)), device_id_type=MESH
+        )
+
+    pl.semaphore_wait(barrier, n - 1)
+    return me
+
+
+def pair_start(occ, k):
+    return k * (occ - 1) - k * (k - 1) // 2
+
+
+def pack_anti(occ, shard, padded, wide, packed):
+    nshards = packed.shape[0] // padded
+    for s in range(nshards):
+        packed[s * padded + shard:(s + 1) * padded, :] = jnp.zeros((padded - shard, LANES), F32)
+    for k in range(occ - 1):
+        row = wide[k * occ:(k + 1) * occ, :]
+        col = wide[pl.ds(k, occ, stride=occ), :]
+        diff = row - col
+        at, end = pair_start(occ, k), pair_start(occ, k + 1)
+        base = k + 1 - at
+        while at < end:
+            s = at // shard
+            stop = min(end, (s + 1) * shard)
+            lift = s * (padded - shard)
+            packed[at + lift:stop + lift, :] = diff[at + base:stop + base, :]
+            at = stop
+
+
+def finish(occ, eps_row, energy, lad, mixed, rf, upd):
+    for i in range(occ):
+        if i == occ - 1:
+            break
+        row = mixed[i * occ:(i + 1) * occ, :]
+        col = mixed[pl.ds(i, occ, stride=occ), :]
+        at, n = pair_start(occ, i), occ - 1 - i
+        diff = (row - col)[i + 1:, :]
+        rf[i * occ + i + 1:(i + 1) * occ, :] = lad[at:at + n, :] - diff
+    second = jnp.broadcast_to(eps_row[...], (LANES, LANES)).T[:occ, :]
+    index = lax.broadcasted_iota(jnp.int32, (occ, LANES), 0)
+    for i in range(occ):
+        row = rf[i * occ:(i + 1) * occ, :]
+        col = rf[pl.ds(i, occ, stride=occ), :]
+        value = jnp.where(index > i, row, jnp.where(index < i, -col, 0.0))
+        denom = (energy - eps_row[0:1, i:i + 1]) - second
+        value = value.astype(BF16).astype(F32)
+        upd[i] = (value / denom).astype(BF16)
+
+
+def fused_kernel(noi, noj, shard, amps, wpad, fock, eps_row, energies, out, pair, wfull, wide, mixed,
+                 packed, left, acc, lad, rf, upd, asend, arecv, zsend, zrecv, xsend, xrecv,
+                 csend, crecv, osend, orecv, own):
+    n = noi * noj
+    bi, bj = amps.shape[0], amps.shape[1]
+    occ = pair.shape[0]
+    nq = noi // 2
+    padded, cols = wpad.shape
+    rows = padded // nq
+    half = cols // 2
+    oi, oj = lax.axis_index("oi"), lax.axis_index("oj")
+    q, core = oi // 2, lax.rem(oi, 2)
+    me = greet_all(noi, noj)
+
+    def part(ref, quarter, side):
+        return ref.at[pl.ds(pl.multiple_of(quarter * rows, rows), rows),
+                      pl.ds(pl.multiple_of(side * half, half), half)]
+
+    def slot(s, quarter, side):
+        return part(wfull.at[s], quarter, side)
+
+    def comes_from(d, h):
+        return oj - h if d == 0 else oj + h
+
+    def gets(d, h):
+        return oj >= h if d == 0 else oj + h < noj
+
+    def can_send(d, h):
+        if d == 0:
+            return jnp.logical_and(oj + 1 < noj, oj + 1 >= h)
+        return jnp.logical_and(oj >= 1, oj + h - 1 < noj)
+
+    def z_copy(d, h):
+        s = oj - h + 1 if d == 0 else oj + h - 1
+        return pltpu.make_async_remote_copy(
+            src_ref=part(wpad, q, core) if h == 1 else slot(s, q, core),
+            dst_ref=slot(s, q, core), send_sem=zsend.at[d, h], recv_sem=zrecv.at[d, h],
+            device_id=spot(oi, oj + 1 if d == 0 else oj - 1), device_id_type=MESH)
+
+    def x_copy(d, h, dq):
+        s = comes_from(d, h)
+        return pltpu.make_async_remote_copy(
+            src_ref=slot(s, q, core), dst_ref=slot(s, q, core),
+            send_sem=xsend.at[d, h, dq], recv_sem=xrecv.at[d, h, dq],
+            device_id=spot(lax.rem(q + dq, nq) * 2 + core, oj), device_id_type=MESH)
+
+    def c_copy(d, h, dq):
+        s = comes_from(d, h)
+        quarter = lax.rem(q + nq - dq, nq)
+        return pltpu.make_async_remote_copy(
+            src_ref=slot(s, quarter, core), dst_ref=slot(s, quarter, core),
+            send_sem=csend.at[d, h, dq], recv_sem=crecv.at[d, h, dq],
+            device_id=spot(q * 2 + 1 - core, oj), device_id_type=MESH)
+
+    def target(peer):
+        return spot(peer // noj, lax.rem(peer, noj))
+
+    def columns(ref, peer):
+        return ref.at[:, :, pl.ds(pl.multiple_of(peer * LANES, LANES), LANES)]
+
+    def block(ref, peer):
+        return ref.at[pl.ds((peer // noj) * bi, bi),
+                      pl.ds(pl.multiple_of(lax.rem(peer, noj) * bj, bj), bj), :]
+
+    def a_copy(t):
+        peer = lax.rem(me + t, n)
+        return pltpu.make_async_remote_copy(
+            src_ref=columns(amps, peer), dst_ref=block(pair, me),
+            send_sem=asend.at[t], recv_sem=arecv.at[t],
+            device_id=target(peer), device_id_type=MESH)
+
+    def o_copy(t):
+        peer = lax.rem(me + t, n)
+        return pltpu.make_async_remote_copy(
+            src_ref=block(upd, peer), dst_ref=columns(out, me),
+            send_sem=osend.at[t], recv_sem=orecv.at[t],
+            device_id=target(peer), device_id_type=MESH)
+
+    def z_start(d, h):
+        @pl.when(can_send(d, h))
+        def _():
+            z_copy(d, h).start()
+
+    for d in range(2):
+        z_start(d, 1)
+
+    @pl.loop(1, n)
+    def _(t):
+        a_copy(t).start()
+
+    mine = pltpu.make_async_copy(columns(amps, me), block(pair, me), own.at[0])
+    mine.start()
+    whole = pltpu.make_async_copy(wpad, wfull.at[oj], own.at[1])
+    whole.start()
+
+    for h in range(1, noj):
+        for d in range(2):
+            @pl.when(gets(d, h))
+            def _():
+                z_copy(d, h).wait_recv()
+            if h + 1 < noj:
+                z_start(d, h + 1)
+
+            @pl.when(gets(d, h))
+            def _():
+                for dq in range(1, nq):
+                    x_copy(d, h, dq).start()
+                c_copy(d, h, 0).start()
+
+    def swap(h):
+        for d in range(2):
+            @pl.when(gets(d, h))
+            def _():
+                for dq in range(1, nq):
+                    x_copy(d, h, dq).wait_recv()
+                    c_copy(d, h, dq).start()
+
+    def multiply(s, first):
+        rows_of = left[:, pl.ds(pl.multiple_of(s * padded, padded), padded)]
+
+        @pl.loop(0, cols // 256)
+        def _(c):
+            at = pl.ds(pl.multiple_of(c * 256, 256), 256)
+            term = jnp.dot(rows_of, wfull[s, :, at], preferred_element_type=F32)
+            if first:
+                acc[:, at] = term
+            else:
+                acc[:, at] += term
+
+    swap(1)
+    mine.wait()
+
+    @pl.loop(1, n)
+    def _(t):
+        a_copy(t).wait_recv()
+
+    flipped = fock[...].astype(F32).T.astype(BF16)
+
+    @pl.loop(0, occ)
+    def _(i):
+        rows_i = pair[i]
+        at = pl.ds(pl.multiple_of(i * occ, occ), occ)
+        wide[at, :] = rows_i.astype(F32)
+        mixed[at, :] = jnp.dot(flipped, rows_i, preferred_element_type=F32)
+
+    pack_anti(occ, shard, padded, wide, packed)
+    left[...] = packed[...].T.astype(BF16)
+    whole.wait()
+    multiply(oj, True)
+    for h in range(1, noj):
+        if h > 1:
+            swap(h)
+        for d in range(2):
+            @pl.when(gets(d, h))
+            def _():
+                for dq in range(nq):
+                    c_copy(d, h, dq).wait_recv()
+                multiply(comes_from(d, h), False)
+
+    @pl.loop(0, cols // 256)
+    def _(c):
+        at = pl.ds(pl.multiple_of(c * 256, 256), 256)
+        lad[at, :] = acc[:, at].T
+
+    finish(occ, eps_row, energies[pl.ds(me, 1), :], lad, mixed, rf, upd)
+
+    @pl.loop(1, n)
+    def _(t):
+        o_copy(t).start()
+
+    last = pltpu.make_async_copy(block(upd, me), columns(out, me), own.at[2])
+    last.start()
+
+    for h in range(1, noj):
+        for d in range(2):
+            @pl.when(can_send(d, h))
+            def _():
+                z_copy(d, h).wait_send()
+
+            @pl.when(gets(d, h))
+            def _():
+                for dq in range(nq):
+                    if dq:
+                        x_copy(d, h, dq).wait_send()
+                    c_copy(d, h, dq).wait_send()
+    last.wait()
+
+    @pl.loop(1, n)
+    def _(t):
+        a_copy(t).wait_send()
+        o_copy(t).wait()
+
+
+def fused(noi, noj, shard, amps, wpad, fock, eps_row, energies):
+    occ = amps.shape[0] * noi
+    padded, cols = wpad.shape
+    dma, vmem = pltpu.SemaphoreType.DMA, pltpu.VMEM
+    line, plane = dma((2, noj)), dma((2, noj, noi // 2))
+    square = vmem((occ * occ, LANES), F32)
+    everyone = dma((noi * noj,))
+    remote, local = pl.BlockSpec(memory_space=pl.ANY), pl.BlockSpec(memory_space=vmem)
+    return pl.pallas_call(
+        functools.partial(fused_kernel, noi, noj, shard),
+        out_shape=jax.ShapeDtypeStruct(amps.shape, BF16),
+        in_specs=[remote, remote, local, local, local],
+        out_specs=remote,
+        scratch_shapes=[
+            vmem((occ, occ, LANES), BF16), vmem((noj, padded, cols), BF16), square, square,
+            vmem((noj * padded, LANES), F32), vmem((LANES, noj * padded), BF16),
+            vmem((LANES, cols), F32), vmem((cols, LANES), F32), square,
+            vmem((occ, occ, LANES), BF16),
+            everyone, everyone, line, line, plane, plane, plane, plane, everyone, everyone,
+            dma((3,)),
+        ],
+        compiler_params=pltpu.CompilerParams(
+            collective_id=0, has_side_effects=True, vmem_limit_bytes=48 * 2**20),
+    )(amps, wpad, fock, eps_row, energies)
+
+
+def up_to(value, unit):
+    return -(-value // unit) * unit
+
+
+def with_kernels(noi, noj, amps, ladder_w, fock, eps_occ, eps_pair):
+    occ = amps.shape[0] * noi
+    shard, cols = ladder_w.shape
+    padded = up_to(shard, 16 * noi // 2)
+    wpad = jnp.pad(ladder_w, ((0, padded - shard), (0, up_to(cols, 256) - cols)))
+    eps_row = jnp.pad(eps_occ, (0, LANES - occ)).reshape(1, LANES)
+    energies = eps_pair.reshape(noi * noj, LANES)
+    return fused(noi, noj, shard, amps, wpad, fock, eps_row, energies)
+
 
 def solution(mesh):
+    noi, noj = mesh.shape["oi"], mesh.shape["oj"]
+
+    def on_device(amps, *rest):
+        fits = amps.shape[1] % 16 == 0 and amps.shape[2] == noi * noj * LANES
+        fits = fits and noi % 2 == 0 and amps.shape[0] * noi <= LANES
+        if fits:
+            return with_kernels(noi, noj, amps, *rest)
+        return with_collectives(amps, *rest)
+
     in_specs = (P("oi", "oj", None), P("oj", None), P(), P(), P())
     out_specs = P("oi", "oj", None)
     return jax.shard_map(

time: 269 us -> 97.8 us (0.36)
  Pallas kernels: 0 us -> 93.9 us
  waiting for transfers between devices: 90 us -> 0 us
  local copies, waits for them, and re-layouts: 75.7 us -> 3.6 us
  blocking collectives: 66.9 us -> 0 us
  between operations: 13.6 us -> 0.04 us
  other arithmetic: 8.86 us -> 0 us
  matrix products: 8.58 us -> 0 us
  starting transfers between devices: 4.83 us -> 0 us
    pallas_call x0 -> x1, Pallas kernels: none -> 93.9 us  [fused(): pl.pallas_call(functools.partial(fused_kernel, noi, noj, shard), out_shap...]
    all_to_all x3 -> x0, blocking collectives: 66.9 us -> none  [the longest x1 27.8 us: on_device(): lax.all_to_all(lax.all_to_all(outgoing, 'oi', split_axis=0, concat_axis=2...]
    all_to_all x1 -> x0, waiting for transfers between devices: 53.4 us -> none  [on_device(): lax.all_to_all(lax.all_to_all(amps, 'oi', split_axis=2, concat_axis=0, ti...]
    all_gather x1 -> x0, waiting for transfers between devices: 35.9 us -> none  [on_device(): whole_w = lax.all_gather(ladder_w, 'oj', axis=0, tiled=True)]
    unnamed x17 -> x7, local copies, waits for them, and re-layouts: 30.3 us -> 0.98 us
    gather x3 -> x0, local copies, waits for them, and re-layouts: 26.8 us -> none  [the longest x1 14.1 us: on_device(): jnp.concatenate([ladder, -ladder, filler], axis=0)[expand]]
    all_to_all x6 -> x0, local copies, waits for them, and re-layouts: 15.5 us -> none  [the longest x2 11 us: on_device(): lax.all_to_all(amps, 'oi', split_axis=2, concat_axis=0, tiled=True)]
    dot_general x2 -> x0, matrix products: 8.58 us -> none  [the longest x1 6.78 us: on_device(): lax.dot_general(whole_w, anti[:, 0:0 + width], contract, preferred_elemen...]
  transfers between devices with their start and end apart: 2 -> 0, of which waited for: 2 -> 0; matrix products, arithmetic and copies ran while one was open for 22% -> 0% of each run, Pallas kernels for 0% -> 0%
where the time goes in v2:
time: 97.8 us; the launch traced here: 97.6 us
  Pallas kernels  93.9 us (96%)
  local copies, waits for them, and re-layouts  3.6 us (4%)
    pallas_call x1, Pallas kernels, fused(): pl.pallas_call(functools.partial(fused_kernel, noi, noj, shard), out_shap...  93.9 us

profile of v2, /device:TPU:0, one launch (start us, length us, event | category | flops | bytes accessed | tf_op | source)
XLA Modules:
  0.0 97.6 jit_solution(17517623727917324492)
XLA Ops:
  0.0 0.0 copy-start.2
  0.0 0.0 copy-start.1
  0.0 0.0 copy-start
  0.0 0.7 pad_bitcast_fusion.eps_row
  0.8 1.9 %pad.8.wpad = bf16[512,2048]{1,0:T(8,128)(2,1)S(1)} pad(bf16[504,2016]{1,0:T(8,128)(2,1)} %param.6, bf16[]{:T(256)} %constant.3.clone.1), padding=0_8x0_32 | pad | bytes 4129282 | tf_op jit(solution)/shard_map/jit(_pad)/pad | solution.py:360
  2.6 0.0 copy-done.2
  2.6 0.0 copy-done.1
  2.6 0.0 copy-done
  2.7 93.9 %shard_map.55 = bf16[8,16,4096]{2,1,0:T(8,128)(2,1)S(1)} custom-call(bf16[8,16,4096]{2,1,0:T(8,128)(2,1)S(1)} %copy-done, bf16[512,2048]{1,0:T(8,128)(2,1)S(1)} %pad.8.wpad, bf16[64,64]{1,0:T(8,128)(2,1)S(1)} %copy-done.1, f32[1,128]{1,0:T(1,128)S(1)} %pad_bitcast_fusion.eps_row, f32[32,128]{1,0:T(8,128)S(1)} %bitcast.3), custom_call_target="tpu_custom_call" | custom-call | tf_op jit(solution)/shard_map/pallas_call | solution.py:334
  96.6 1.0 copy.7
Async XLA Ops:
  0.0 2.6 %copy-start.2 = (f32[4096]{0:T(1024)S(1)}, f32[4096]{0:T(1024)}, u32[]{:S(2)}) copy-start(f32[4096]{0:T(1024)} %param.9) | copy-start | bytes 49156
  0.0 2.6 %copy-start.1 = (bf16[64,64]{1,0:T(8,128)(2,1)S(1)}, bf16[64,64]{1,0:T(8,128)(2,1)}, u32[]{:S(2)}) copy-start(bf16[64,64]{1,0:T(8,128)(2,1)} %fock.1) | copy-start | bytes 24580
  0.0 2.6 %copy-start = (bf16[8,16,4096]{2,1,0:T(8,128)(2,1)S(1)}, bf16[8,16,4096]{2,1,0:T(8,128)(2,1)}, u32[]{:S(2)}) copy-start(bf16[8,16,4096]{2,1,0:T(8,128)(2,1)} %amps.1) | copy-start | bytes 3145732

commit v3 on v2

--- a/solution.py
+++ b/solution.py
@@ -110,24 +110,32 @@
             at = stop
 
 
-def finish(occ, eps_row, energy, lad, mixed, rf, upd):
-    for i in range(occ):
-        if i == occ - 1:
-            break
+def residual(occ, low, high, lad, mixed, rf):
+    for i in range(low, high):
         row = mixed[i * occ:(i + 1) * occ, :]
         col = mixed[pl.ds(i, occ, stride=occ), :]
         at, n = pair_start(occ, i), occ - 1 - i
         diff = (row - col)[i + 1:, :]
         rf[i * occ + i + 1:(i + 1) * occ, :] = lad[at:at + n, :] - diff
+
+
+def divide(occ, start, full, cut, eps_row, energy, rf, upd):
     second = jnp.broadcast_to(eps_row[...], (LANES, LANES)).T[:occ, :]
     index = lax.broadcasted_iota(jnp.int32, (occ, LANES), 0)
-    for i in range(occ):
-        row = rf[i * occ:(i + 1) * occ, :]
-        col = rf[pl.ds(i, occ, stride=occ), :]
-        value = jnp.where(index > i, row, jnp.where(index < i, -col, 0.0))
-        denom = (energy - eps_row[0:1, i:i + 1]) - second
+    for i in range(start, occ):
+        low, high = (0, occ if i < full else cut) if start == 0 else (cut, occ)
+        if low == high:
+            continue
+        denom = (energy - eps_row[0:1, i:i + 1]) - second[low:high, :]
+        col = rf[pl.ds(low * occ + i, high - low, stride=occ), :]
+        if high <= i:
+            value = -col
+        else:
+            row = rf[i * occ + low:i * occ + high, :]
+            at = index[low:high, :]
+            value = jnp.where(at > i, row, jnp.where(at < i, -col, 0.0))
         value = value.astype(BF16).astype(F32)
-        upd[i] = (value / denom).astype(BF16)
+        upd[i, low:high, :] = (value / denom).astype(BF16)
 
 
 def fused_kernel(noi, noj, shard, amps, wpad, fock, eps_row, energies, out, pair, wfull, wide, mixed,
@@ -140,16 +148,17 @@
     padded, cols = wpad.shape
     rows = padded // nq
     half = cols // 2
+    side_cols = half // 2
     oi, oj = lax.axis_index("oi"), lax.axis_index("oj")
     q, core = oi // 2, lax.rem(oi, 2)
     me = greet_all(noi, noj)
 
-    def part(ref, quarter, side):
-        return ref.at[pl.ds(pl.multiple_of(quarter * rows, rows), rows),
-                      pl.ds(pl.multiple_of(side * half, half), half)]
-
-    def slot(s, quarter, side):
-        return part(wfull.at[s], quarter, side)
+    def part(ref, quarter, side, p):
+        at = pl.multiple_of(p * half + side * side_cols, side_cols)
+        return ref.at[pl.ds(pl.multiple_of(quarter * rows, rows), rows), pl.ds(at, side_cols)]
+
+    def slot(s, quarter, side, p):
+        return part(wfull.at[s], quarter, side, p)
 
     def comes_from(d, h):
         return oj - h if d == 0 else oj + h
@@ -162,26 +171,26 @@
             return jnp.logical_and(oj + 1 < noj, oj + 1 >= h)
         return jnp.logical_and(oj >= 1, oj + h - 1 < noj)
 
-    def z_copy(d, h):
+    def z_copy(p, d, h):
         s = oj - h + 1 if d == 0 else oj + h - 1
         return pltpu.make_async_remote_copy(
-            src_ref=part(wpad, q, core) if h == 1 else slot(s, q, core),
-            dst_ref=slot(s, q, core), send_sem=zsend.at[d, h], recv_sem=zrecv.at[d, h],
+            src_ref=part(wpad, q, core, p) if h == 1 else slot(s, q, core, p),
+            dst_ref=slot(s, q, core, p),
+            send_sem=zsend.at[2 * p + d, h], recv_sem=zrecv.at[2 * p + d, h],
             device_id=spot(oi, oj + 1 if d == 0 else oj - 1), device_id_type=MESH)
 
-    def x_copy(d, h, dq):
-        s = comes_from(d, h)
+    def x_copy(p, d, h, dq):
+        ref = slot(comes_from(d, h), q, core, p)
         return pltpu.make_async_remote_copy(
-            src_ref=slot(s, q, core), dst_ref=slot(s, q, core),
-            send_sem=xsend.at[d, h, dq], recv_sem=xrecv.at[d, h, dq],
+            src_ref=ref, dst_ref=ref,
+            send_sem=xsend.at[2 * p + d, h, dq], recv_sem=xrecv.at[2 * p + d, h, dq],
             device_id=spot(lax.rem(q + dq, nq) * 2 + core, oj), device_id_type=MESH)
 
-    def c_copy(d, h, dq):
-        s = comes_from(d, h)
-        quarter = lax.rem(q + nq - dq, nq)
+    def c_copy(p, d, h, dq):
+        ref = slot(comes_from(d, h), lax.rem(q + nq - dq, nq), core, p)
         return pltpu.make_async_remote_copy(
-            src_ref=slot(s, quarter, core), dst_ref=slot(s, quarter, core),
-            send_sem=csend.at[d, h, dq], recv_sem=crecv.at[d, h, dq],
+            src_ref=ref, dst_ref=ref,
+            send_sem=csend.at[2 * p + d, h, dq], recv_sem=crecv.at[2 * p + d, h, dq],
             device_id=spot(q * 2 + 1 - core, oj), device_id_type=MESH)
 
     def target(peer):
@@ -208,13 +217,14 @@
             send_sem=osend.at[t], recv_sem=orecv.at[t],
             device_id=target(peer), device_id_type=MESH)
 
-    def z_start(d, h):
+    def z_start(p, d, h):
         @pl.when(can_send(d, h))
         def _():
-            z_copy(d, h).start()
-
-    for d in range(2):
-        z_start(d, 1)
+            z_copy(p, d, h).start()
+
+    for p in range(2):
+        for d in range(2):
+            z_start(p, d, 1)
 
     @pl.loop(1, n)
     def _(t):
@@ -225,32 +235,32 @@
     whole = pltpu.make_async_copy(wpad, wfull.at[oj], own.at[1])
     whole.start()
 
-    for h in range(1, noj):
+    def arrive(p, h):
         for d in range(2):
             @pl.when(gets(d, h))
             def _():
-                z_copy(d, h).wait_recv()
+                z_copy(p, d, h).wait_recv()
             if h + 1 < noj:
-                z_start(d, h + 1)
+                z_start(p, d, h + 1)
 
             @pl.when(gets(d, h))
             def _():
                 for dq in range(1, nq):
-                    x_copy(d, h, dq).start()
-                c_copy(d, h, 0).start()
-
-    def swap(h):
+                    x_copy(p, d, h, dq).start()
+                c_copy(p, d, h, 0).start()
+
+    def swap(p, h):
         for d in range(2):
             @pl.when(gets(d, h))
             def _():
                 for dq in range(1, nq):
-                    x_copy(d, h, dq).wait_recv()
-                    c_copy(d, h, dq).start()
-
-    def multiply(s, first):
+                    x_copy(p, d, h, dq).wait_recv()
+                    c_copy(p, d, h, dq).start()
+
+    def multiply(p, s, first):
         rows_of = left[:, pl.ds(pl.multiple_of(s * padded, padded), padded)]
 
-        @pl.loop(0, cols // 256)
+        @pl.loop(p * half // 256, (p + 1) * half // 256)
         def _(c):
             at = pl.ds(pl.multiple_of(c * 256, 256), 256)
             term = jnp.dot(rows_of, wfull[s, :, at], preferred_element_type=F32)
@@ -259,7 +269,24 @@
             else:
                 acc[:, at] += term
 
-    swap(1)
+    def ladder(p):
+        for h in range(1, noj):
+            swap(p, h)
+            for d in range(2):
+                @pl.when(gets(d, h))
+                def _():
+                    for dq in range(nq):
+                        c_copy(p, d, h, dq).wait_recv()
+                    multiply(p, comes_from(d, h), False)
+
+        @pl.loop(p * half // 256, (p + 1) * half // 256)
+        def _(c):
+            at = pl.ds(pl.multiple_of(c * 256, 256), 256)
+            lad[at, :] = acc[:, at].T
+
+    for h in range(1, noj):
+        for p in range(2):
+            arrive(p, h)
     mine.wait()
 
     @pl.loop(1, n)
@@ -278,43 +305,48 @@
     pack_anti(occ, shard, padded, wide, packed)
     left[...] = packed[...].T.astype(BF16)
     whole.wait()
-    multiply(oj, True)
-    for h in range(1, noj):
-        if h > 1:
-            swap(h)
-        for d in range(2):
-            @pl.when(gets(d, h))
+    multiply(0, oj, True)
+    multiply(1, oj, True)
+
+    unit = max(bi, bj)
+    early = max(e for e in range(0, occ, unit) if pair_start(occ, e) <= half)
+    energy = energies[pl.ds(me, 1), :]
+
+    def send(now):
+        @pl.loop(1, n)
+        def _(t):
+            peer = lax.rem(me + t, n)
+            soon = jnp.logical_or(peer // noj < early // bi, lax.rem(peer, noj) < early // bj)
+
+            @pl.when(soon if now else jnp.logical_not(soon))
             def _():
-                for dq in range(nq):
-                    c_copy(d, h, dq).wait_recv()
-                multiply(comes_from(d, h), False)
-
-    @pl.loop(0, cols // 256)
-    def _(c):
-        at = pl.ds(pl.multiple_of(c * 256, 256), 256)
-        lad[at, :] = acc[:, at].T
-
-    finish(occ, eps_row, energies[pl.ds(me, 1), :], lad, mixed, rf, upd)
-
-    @pl.loop(1, n)
-    def _(t):
-        o_copy(t).start()
+                o_copy(t).start()
+
+    ladder(0)
+    residual(occ, 0, early, lad, mixed, rf)
+    divide(occ, 0, early, early, eps_row, energy, rf, upd)
+    send(True)
+    ladder(1)
+    residual(occ, early, occ - 1, lad, mixed, rf)
+    divide(occ, early, 0, early, eps_row, energy, rf, upd)
+    send(False)
 
     last = pltpu.make_async_copy(block(upd, me), columns(out, me), own.at[2])
     last.start()
 
-    for h in range(1, noj):
-        for d in range(2):
-            @pl.when(can_send(d, h))
-            def _():
-                z_copy(d, h).wait_send()
-
-            @pl.when(gets(d, h))
-            def _():
-                for dq in range(nq):
-                    if dq:
-                        x_copy(d, h, dq).wait_send()
-                    c_copy(d, h, dq).wait_send()
+    for p in range(2):
+        for h in range(1, noj):
+            for d in range(2):
+                @pl.when(can_send(d, h))
+                def _():
+                    z_copy(p, d, h).wait_send()
+
+                @pl.when(gets(d, h))
+                def _():
+                    for dq in range(nq):
+                        if dq:
+                            x_copy(p, d, h, dq).wait_send()
+                        c_copy(p, d, h, dq).wait_send()
     last.wait()
 
     @pl.loop(1, n)
@@ -327,7 +359,7 @@
     occ = amps.shape[0] * noi
     padded, cols = wpad.shape
     dma, vmem = pltpu.SemaphoreType.DMA, pltpu.VMEM
-    line, plane = dma((2, noj)), dma((2, noj, noi // 2))
+    line, plane = dma((4, noj)), dma((4, noj, noi // 2))
     square = vmem((occ * occ, LANES), F32)
     everyone = dma((noi * noj,))
     remote, local = pl.BlockSpec(memory_space=pl.ANY), pl.BlockSpec(memory_space=vmem)
@@ -357,7 +389,7 @@
     occ = amps.shape[0] * noi
     shard, cols = ladder_w.shape
     padded = up_to(shard, 16 * noi // 2)
-    wpad = jnp.pad(ladder_w, ((0, padded - shard), (0, up_to(cols, 256) - cols)))
+    wpad = jnp.pad(ladder_w, ((0, padded - shard), (0, up_to(cols, 512) - cols)))
     eps_row = jnp.pad(eps_occ, (0, LANES - occ)).reshape(1, LANES)
     energies = eps_pair.reshape(noi * noj, LANES)
     return fused(noi, noj, shard, amps, wpad, fock, eps_row, energies)

time: 97.8 us -> 94.4 us (0.965)
  Pallas kernels: 93.9 us -> 90.6 us
    pallas_call x1, Pallas kernels: 93.9 us -> 90.6 us  [fused(): pl.pallas_call(functools.partial(fused_kernel, noi, noj, shard), out_shap...]
where the time goes in v3:
time: 94.4 us; the launch traced here: 94.3 us
  Pallas kernels  90.6 us (96%)
  local copies, waits for them, and re-layouts  3.6 us (4%)
    pallas_call x1, Pallas kernels, fused(): pl.pallas_call(functools.partial(fused_kernel, noi, noj, shard), out_shap...  90.6 us

profile of v3, /device:TPU:0, one launch (start us, length us, event | category | flops | bytes accessed | tf_op | source)
XLA Modules:
  0.0 94.3 jit_solution(6742606846419403856)
XLA Ops:
  0.0 0.0 copy-start.2
  0.0 0.0 copy-start.1
  0.0 0.0 copy-start
  0.0 0.7 pad_bitcast_fusion.eps_row
  0.8 1.9 %pad.8.wpad = bf16[512,2048]{1,0:T(8,128)(2,1)S(1)} pad(bf16[504,2016]{1,0:T(8,128)(2,1)} %param.6, bf16[]{:T(256)} %constant.3.clone.1), padding=0_8x0_32 | pad | bytes 4129282 | tf_op jit(solution)/shard_map/jit(_pad)/pad | solution.py:392
  2.6 0.0 copy-done.2
  2.6 0.0 copy-done.1
  2.6 0.0 copy-done
  2.7 90.6 %shard_map.55 = bf16[8,16,4096]{2,1,0:T(8,128)(2,1)S(1)} custom-call(bf16[8,16,4096]{2,1,0:T(8,128)(2,1)S(1)} %copy-done, bf16[512,2048]{1,0:T(8,128)(2,1)S(1)} %pad.8.wpad, bf16[64,64]{1,0:T(8,128)(2,1)S(1)} %copy-done.1, f32[1,128]{1,0:T(1,128)S(1)} %pad_bitcast_fusion.eps_row, f32[32,128]{1,0:T(8,128)S(1)} %bitcast.3), custom_call_target="tpu_custom_call" | custom-call | tf_op jit(solution)/shard_map/pallas_call | solution.py:366
  93.3 1.0 %copy.7 = bf16[8,16,4096]{2,1,0:T(8,128)(2,1)} copy(bf16[8,16,4096]{2,1,0:T(8,128)(2,1)S(1)} %shard_map.55) | data formatting | bytes 2097152
Async XLA Ops:
  0.0 2.6 %copy-start.2 = (f32[4096]{0:T(1024)S(1)}, f32[4096]{0:T(1024)}, u32[]{:S(2)}) copy-start(f32[4096]{0:T(1024)} %param.9) | copy-start | bytes 49156
  0.0 2.6 %copy-start.1 = (bf16[64,64]{1,0:T(8,128)(2,1)S(1)}, bf16[64,64]{1,0:T(8,128)(2,1)}, u32[]{:S(2)}) copy-start(bf16[64,64]{1,0:T(8,128)(2,1)} %fock.1) | copy-start | bytes 24580
  0.0 2.6 %copy-start = (bf16[8,16,4096]{2,1,0:T(8,128)(2,1)S(1)}, bf16[8,16,4096]{2,1,0:T(8,128)(2,1)}, u32[]{:S(2)}) copy-start(bf16[8,16,4096]{2,1,0:T(8,128)(2,1)} %amps.1) | copy-start | bytes 3145732

commit v4 on v3

--- a/solution.py
+++ b/solution.py
@@ -306,7 +306,6 @@
     left[...] = packed[...].T.astype(BF16)
     whole.wait()
     multiply(0, oj, True)
-    multiply(1, oj, True)
 
     unit = max(bi, bj)
     early = max(e for e in range(0, occ, unit) if pair_start(occ, e) <= half)
@@ -326,6 +325,7 @@
     residual(occ, 0, early, lad, mixed, rf)
     divide(occ, 0, early, early, eps_row, energy, rf, upd)
     send(True)
+    multiply(1, oj, True)
     ladder(1)
     residual(occ, early, occ - 1, lad, mixed, rf)
     divide(occ, early, 0, early, eps_row, energy, rf, upd)

time: 94.4 us -> 94.4 us (level)
  no operation moved by 1% of the time
where the time goes in v4:
time: 94.4 us; the launch traced here: 94.3 us
  Pallas kernels  90.6 us (96%)
  local copies, waits for them, and re-layouts  3.6 us (4%)
    pallas_call x1, Pallas kernels, fused(): pl.pallas_call(functools.partial(fused_kernel, noi, noj, shard), out_shap...  90.6 us

profile of v4, /device:TPU:0, one launch (start us, length us, event | category | flops | bytes accessed | tf_op | source)
XLA Modules:
  0.0 94.3 jit_solution(11993894528345707282)
XLA Ops:
  0.0 0.0 copy-start.2
  0.0 0.0 copy-start.1
  0.0 0.0 copy-start
  0.0 0.7 pad_bitcast_fusion.eps_row
  0.8 1.9 %pad.8.wpad = bf16[512,2048]{1,0:T(8,128)(2,1)S(1)} pad(bf16[504,2016]{1,0:T(8,128)(2,1)} %param.6, bf16[]{:T(256)} %constant.3.clone.1), padding=0_8x0_32 | pad | bytes 4129282 | tf_op jit(solution)/shard_map/jit(_pad)/pad | solution.py:392
  2.6 0.0 copy-done.2
  2.6 0.0 copy-done.1
  2.6 0.0 copy-done
  2.7 90.6 %shard_map.55 = bf16[8,16,4096]{2,1,0:T(8,128)(2,1)S(1)} custom-call(bf16[8,16,4096]{2,1,0:T(8,128)(2,1)S(1)} %copy-done, bf16[512,2048]{1,0:T(8,128)(2,1)S(1)} %pad.8.wpad, bf16[64,64]{1,0:T(8,128)(2,1)S(1)} %copy-done.1, f32[1,128]{1,0:T(1,128)S(1)} %pad_bitcast_fusion.eps_row, f32[32,128]{1,0:T(8,128)S(1)} %bitcast.3), custom_call_target="tpu_custom_call" | custom-call | tf_op jit(solution)/shard_map/pallas_call | solution.py:366
  93.3 1.0 %copy.7 = bf16[8,16,4096]{2,1,0:T(8,128)(2,1)} copy(bf16[8,16,4096]{2,1,0:T(8,128)(2,1)S(1)} %shard_map.55) | data formatting | bytes 2097152
Async XLA Ops:
  0.0 2.6 %copy-start.2 = (f32[4096]{0:T(1024)S(1)}, f32[4096]{0:T(1024)}, u32[]{:S(2)}) copy-start(f32[4096]{0:T(1024)} %param.9) | copy-start | bytes 49156
  0.0 2.6 %copy-start.1 = (bf16[64,64]{1,0:T(8,128)(2,1)S(1)}, bf16[64,64]{1,0:T(8,128)(2,1)}, u32[]{:S(2)}) copy-start(bf16[64,64]{1,0:T(8,128)(2,1)} %fock.1) | copy-start | bytes 24580
  0.0 2.6 %copy-start = (bf16[8,16,4096]{2,1,0:T(8,128)(2,1)S(1)}, bf16[8,16,4096]{2,1,0:T(8,128)(2,1)}, u32[]{:S(2)}) copy-start(bf16[8,16,4096]{2,1,0:T(8,128)(2,1)} %amps.1) | copy-start | bytes 3145732
